TPU v7x, 32 devices: a whole 2x2x4 slice. The times are simulated.
32 devices in a mesh: wide: 4 (over z), batch: 8 (over y, x, core).
Axes of the slice: x: 2, y: 2, z: 4, core: 2. Of those that a mesh axis runs over, the one named last changes fastest.
Arguments:
- series: bfloat16 [64, 1056, 64], P('batch', 'wide'), may hold values from -60 to 60
- lengths: int32 [64], P('batch'), may hold values from 792 to 1056, as said below
- freqs: int32 [5], replicated, may hold values from 2 to 528, as said below
- cotangent: bfloat16 [64, 1056, 64], P('batch', 'wide'), may hold values from -6 to 6
- kernels: float32 [2342912], P(('wide', 'batch')), may hold values from -0.25 to 0.25
- kernel_m: float32 [2342912], P(('wide', 'batch')), may hold values from -0.0004272461 to 0.0004272461
- kernel_v: float32 [2342912], P(('wide', 'batch')), may hold values from 2.1338632e-10 to 3.4141812e-09
- small: float32 [256], replicated, may hold values from -2 to 2
- small_m: float32 [256], replicated, may hold values from -0.0012207031 to 0.0012207031
- small_v: float32 [256], replicated, may hold values from 8.535453e-10 to 1.2803179e-08
Outputs:
- output: bfloat16 [64, 1056, 64], P('batch', 'wide')
- grad_series: bfloat16 [64, 1056, 64], P('batch', 'wide')
- grad_norm: float32 [], replicated
- new_kernels: float32 [2342912], P(('wide', 'batch'))
- new_kernel_m: float32 [2342912], P(('wide', 'batch'))
- new_kernel_v: float32 [2342912], P(('wide', 'batch'))
- new_small: float32 [256], replicated
- new_small_m: float32 [256], replicated
- new_small_v: float32 [256], replicated
Inputs may be any that keep to these rules, and one draw needn't show every extreme that they name: `freqs`: 5 different divisors of 1056, among them 2 and 528. `lengths`: among the 8 series of each batch index one has length 1056 and one has length 792.
All inputs are finite; a program needn't handle non-finite values.
Results may differ from a plain program's by a relative error of at most 0.0037.
Values may be sent and summed in bfloat16 or wider, within the bound.
A program may use at most 320 MiB of HBM per device.

v0:
```python
import math

import jax
import jax.numpy as jnp
import numpy as np
from jax import lax
from jax.sharding import PartitionSpec as P

C = 64
FF = 64
K = 5
NKER = 6
STEP = 10
SPAN = 11
HALF = 5
TAPS = 286


precise = lax.Precision.HIGHEST
beta_one = 0.9
beta_two = 0.999
learn_rate = 0.1
weight_decay = 0.01
adam_eps = 1e-08
clip_norm = 1.0
norm_eps = 1e-05
inv_root_two = 1.0 / math.sqrt(2.0)
inv_root_tau = 1.0 / math.sqrt(2.0 * math.pi)


def tap_table():
    table = np.zeros((SPAN * SPAN, TAPS), np.float32)
    column = 0
    for kernel in range(NKER):
        for row_off in range(-kernel, kernel + 1):
            for col_off in range(-kernel, kernel + 1):
                table[(row_off + HALF) * SPAN + col_off + HALF, column] = 1.0 / NKER
                column += 1
    return table


def column_shifts(values, period):
    length = values.shape[1]
    padded = jnp.pad(values, ((0, 0), (HALF, HALF), (0, 0)))
    within = jnp.arange(length, dtype=jnp.int32) % period
    pieces = []
    for col_off in range(-HALF, HALF + 1):
        inside = (within + col_off >= 0) & (within + col_off < period)
        shifted = padded[:, HALF + col_off : HALF + col_off + length, :]
        pieces.append(jnp.where(inside[None, :, None], shifted, jnp.zeros_like(shifted)))
    return jnp.concatenate(pieces, axis=2)


def rows_sum(spread, period):
    length = spread.shape[1]
    positions = jnp.arange(length, dtype=jnp.int32)
    summed = jnp.zeros((spread.shape[0], length, spread.shape[3]), jnp.float32)
    for row_off in range(-HALF, HALF + 1):
        source = positions + row_off * period
        inside = (source >= 0) & (source < length)
        rolled = jnp.roll(spread[:, :, row_off + HALF, :], -row_off * period, axis=1)
        summed = summed + jnp.where(inside[None, :, None], rolled, jnp.zeros_like(rolled))
    return summed


def rows_stack(values, period):
    length = values.shape[1]
    positions = jnp.arange(length, dtype=jnp.int32)
    pieces = []
    for row_off in range(-HALF, HALF + 1):
        source = positions - row_off * period
        inside = (source >= 0) & (source < length)
        rolled = jnp.roll(values, row_off * period, axis=1)
        pieces.append(jnp.where(inside[None, :, None], rolled, jnp.zeros_like(rolled)))
    return jnp.concatenate(pieces, axis=2)


def conv_apply(shifted, matrix, period, chan_out):
    spread = jnp.einsum("slk,km->slm", shifted, matrix, preferred_element_type=jnp.float32)
    spread = spread.reshape(shifted.shape[0], shifted.shape[1], SPAN, chan_out)
    return rows_sum(spread, period)


def forward_matrix(merged, chan_in, chan_out):
    grid = merged.reshape(SPAN, SPAN, chan_in, chan_out)
    return grid.transpose(1, 2, 0, 3).reshape(SPAN * chan_in, SPAN * chan_out)


def flipped_matrix(merged, chan_in, chan_out):
    grid = merged.reshape(SPAN, SPAN, chan_in, chan_out)[::-1, ::-1]
    return grid.transpose(1, 3, 0, 2).reshape(SPAN * chan_out, SPAN * chan_in)


def from_gradient_matrix(gradient, chan_in, chan_out):
    grid = gradient.reshape(SPAN, chan_in, SPAN, chan_out)
    return grid.transpose(2, 0, 1, 3).reshape(SPAN * SPAN, chan_in, chan_out)


def expand_taps(table, grad_mat_one, grad_mat_two):
    taps_grad_one = jnp.einsum(
        "xt,xio->tio", table, from_gradient_matrix(grad_mat_one, C, FF), precision=precise
    )
    taps_grad_two = jnp.einsum(
        "xt,xio->tio", table, from_gradient_matrix(grad_mat_two, FF, C), precision=precise
    )
    return jnp.concatenate([taps_grad_one.reshape(-1), taps_grad_two.reshape(-1)])


def spectrum_tables(freqs, positions, length):
    turns = positions[:, None] * freqs[None, :] % length
    angle = turns.astype(jnp.float32) * (2.0 * math.pi / length)
    return (jnp.cos(angle), jnp.sin(angle))


def gelu_slope(values):
    return (
        0.5 * (1.0 + lax.erf(values * inv_root_two))
        + values * jnp.exp(-0.5 * values * values) * inv_root_tau
    )


def adam_update(param, grad, first, second):
    first_new = beta_one * first + (1.0 - beta_one) * grad
    second_new = beta_two * second + (1.0 - beta_two) * grad * grad
    first_hat = first_new / (1.0 - beta_one**STEP)
    second_hat = second_new / (1.0 - beta_two**STEP)
    param_new = param - learn_rate * (
        first_hat / (jnp.sqrt(second_hat) + adam_eps) + weight_decay * param
    )
    return (param_new, first_new, second_new)


def local(series, lengths, freqs, cotangent, kernels, kernel_m, kernel_v, small, small_m, small_v):
    table = jnp.asarray(tap_table())
    whole_kernels = lax.all_gather(kernels, ("wide", "batch"), axis=0, tiled=True)
    split_at = TAPS * C * FF
    merged_one = jnp.einsum(
        "xt,tio->xio", table, whole_kernels[:split_at].reshape(TAPS, C, FF), precision=precise
    )
    merged_two = jnp.einsum(
        "xt,tio->xio", table, whole_kernels[split_at:].reshape(TAPS, FF, C), precision=precise
    )
    matrix_one = forward_matrix(merged_one, C, FF).astype(jnp.bfloat16)
    matrix_two = forward_matrix(merged_two, FF, C).astype(jnp.bfloat16)
    flip_one = flipped_matrix(merged_one, C, FF).astype(jnp.bfloat16)
    flip_two = flipped_matrix(merged_two, FF, C).astype(jnp.bfloat16)
    bias_one = small[:FF]
    bias_two = small[FF : FF + C]
    gain = small[FF + C : FF + 2 * C]
    ln_shift = small[FF + 2 * C :]
    wide_count = lax.axis_size("wide")
    wide_index = lax.axis_index("wide")
    group_series = series.shape[0]
    shard_len = series.shape[1]
    local_series = group_series // wide_count
    length = shard_len * wide_count
    first_row = wide_index * local_series
    local_pos = wide_index * shard_len + jnp.arange(shard_len, dtype=jnp.int32)
    local_valid = local_pos[None, :] < lengths[:, None]
    masked_shard = jnp.where(local_valid[:, :, None], series, jnp.zeros_like(series)).astype(
        jnp.float32
    )
    cos_part, sin_part = spectrum_tables(freqs, local_pos, length)
    partial_real = jnp.einsum("slc,lk->skc", masked_shard, cos_part, precision=precise)
    partial_imag = jnp.einsum("slc,lk->skc", masked_shard, sin_part, precision=precise)
    summed_real, summed_imag = lax.psum((partial_real, partial_imag), "wide")
    real_part = lax.dynamic_slice_in_dim(summed_real, first_row, local_series, 0) * (2.0 / length)
    imag_part = lax.dynamic_slice_in_dim(summed_imag, first_row, local_series, 0) * (2.0 / length)
    whole_x, whole_cot = (
        lax.all_to_all(series, "wide", split_axis=0, concat_axis=1, tiled=True),
        lax.all_to_all(cotangent, "wide", split_axis=0, concat_axis=1, tiled=True),
    )
    own_lengths = lax.dynamic_slice_in_dim(lengths, first_row, local_series, 0)
    positions = jnp.arange(length, dtype=jnp.int32)
    valid = positions[None, :] < own_lengths[:, None]
    masked = jnp.where(valid[:, :, None], whole_x, jnp.zeros_like(whole_x))
    masked_wide = masked.astype(jnp.float32)
    cos_table, sin_table = spectrum_tables(freqs, positions, length)
    magnitude = jnp.sqrt(real_part * real_part + imag_part * imag_part + 1.0)
    branch_weights = jax.nn.softmax(jnp.mean(magnitude, axis=2), axis=1)
    periods = length // freqs
    merged = masked_wide
    kept_input = []
    kept_act = []
    kept_hidden = []
    kept_branch = []
    for which in range(K):
        period = periods[which]
        shifted_input = column_shifts(masked, period)
        hidden_pre = conv_apply(shifted_input, matrix_one, period, FF) + bias_one
        activated = jax.nn.gelu(hidden_pre, approximate=False).astype(jnp.bfloat16)
        shifted_act = column_shifts(activated, period)
        branch = conv_apply(shifted_act, matrix_two, period, C) + bias_two
        merged = merged + branch_weights[:, which, None, None] * branch
        kept_input.append(shifted_input)
        kept_act.append(shifted_act)
        kept_hidden.append(hidden_pre)
        kept_branch.append(branch)
    centered = merged - jnp.mean(merged, axis=2, keepdims=True)
    inverse = lax.rsqrt(jnp.mean(centered * centered, axis=2, keepdims=True) + norm_eps)
    normed = centered * inverse
    valid_wide = valid[:, :, None]
    output_whole = jnp.where(valid_wide, normed * gain + ln_shift, 0.0).astype(jnp.bfloat16)
    grad_out = jnp.where(valid_wide, whole_cot.astype(jnp.float32), 0.0)
    grad_gain = jnp.sum(grad_out * normed, axis=(0, 1))
    grad_shift = jnp.sum(grad_out, axis=(0, 1))
    grad_normed = grad_out * gain
    grad_merged = inverse * (
        grad_normed
        - jnp.mean(grad_normed, axis=2, keepdims=True)
        - normed * jnp.mean(grad_normed * normed, axis=2, keepdims=True)
    )
    grad_input = grad_merged
    grad_mat_one = jnp.zeros((SPAN * C, SPAN * FF), jnp.float32)
    grad_mat_two = jnp.zeros((SPAN * FF, SPAN * C), jnp.float32)
    grad_bias_one = jnp.zeros((FF,), jnp.float32)
    grad_bias_two = jnp.zeros((C,), jnp.float32)
    weight_terms = []
    for which in range(K):
        period = periods[which]
        weight_terms.append(jnp.sum(grad_merged * kept_branch[which], axis=(1, 2)))
        grad_branch = (branch_weights[:, which, None, None] * grad_merged).astype(jnp.bfloat16)
        grad_bias_two = grad_bias_two + jnp.sum(grad_branch.astype(jnp.float32), axis=(0, 1))
        grad_mat_two = grad_mat_two + jnp.einsum(
            "slk,slm->km",
            kept_act[which],
            rows_stack(grad_branch, period),
            preferred_element_type=jnp.float32,
        )
        grad_act = conv_apply(column_shifts(grad_branch, period), flip_two, period, FF)
        grad_hidden = (grad_act * gelu_slope(kept_hidden[which])).astype(jnp.bfloat16)
        grad_bias_one = grad_bias_one + jnp.sum(grad_hidden.astype(jnp.float32), axis=(0, 1))
        grad_mat_one = grad_mat_one + jnp.einsum(
            "slk,slm->km",
            kept_input[which],
            rows_stack(grad_hidden, period),
            preferred_element_type=jnp.float32,
        )
        grad_input = grad_input + conv_apply(
            column_shifts(grad_hidden, period), flip_one, period, C
        )
    grad_weights = jnp.stack(weight_terms, axis=1)
    grad_score = branch_weights * (
        grad_weights - jnp.sum(branch_weights * grad_weights, axis=1, keepdims=True)
    )
    coeff = grad_score[:, :, None] / (magnitude * C)
    grad_input = grad_input + 2.0 / length * (
        jnp.einsum("skc,lk->slc", coeff * real_part, cos_table, precision=precise)
        + jnp.einsum("skc,lk->slc", coeff * imag_part, sin_table, precision=precise)
    )
    grad_whole = jnp.where(valid_wide, grad_input.astype(jnp.bfloat16), jnp.zeros((), jnp.bfloat16))
    output_shards, grad_shards = (
        lax.all_to_all(output_whole, "wide", split_axis=1, concat_axis=0, tiled=True),
        lax.all_to_all(grad_whole, "wide", split_axis=1, concat_axis=0, tiled=True),
    )
    small_grad = jnp.concatenate([grad_bias_one, grad_bias_two, grad_gain, grad_shift])
    local_share = kernels.shape[0]
    owner = lax.axis_index(("wide", "batch"))
    flat_grad = expand_taps(table, grad_mat_one, grad_mat_two)
    full_grad, small_sum = lax.psum((flat_grad, small_grad), ("wide", "batch"))
    square_sum = jnp.sum(full_grad * full_grad) + jnp.sum(small_sum * small_sum)
    share_grad = lax.dynamic_slice_in_dim(full_grad, owner * local_share, local_share)
    grad_norm = jnp.sqrt(square_sum)
    factor = jnp.minimum(1.0, clip_norm / (grad_norm + 1e-06))
    new_kernels, new_kernel_m, new_kernel_v = adam_update(
        kernels, share_grad * factor, kernel_m, kernel_v
    )
    new_small, new_small_m, new_small_v = adam_update(small, small_sum * factor, small_m, small_v)
    return (
        output_shards,
        grad_shards,
        grad_norm,
        new_kernels,
        new_kernel_m,
        new_kernel_v,
        new_small,
        new_small_m,
        new_small_v,
    )


def solution(mesh):
    placed = (
        P("batch", "wide", None),
        P("batch"),
        P(),
        P("batch", "wide", None),
        P(("wide", "batch")),
        P(("wide", "batch")),
        P(("wide", "batch")),
        P(),
        P(),
        P(),
    )
    return jax.shard_map(
        local,
        mesh=mesh,
        in_specs=placed,
        out_specs=(
            P("batch", "wide", None),
            P("batch", "wide", None),
            P(),
            P(("wide", "batch")),
            P(("wide", "batch")),
            P(("wide", "batch")),
            P(),
            P(),
            P(),
        ),
        check_vma=False,
    )
```

profile of v0, /device:TPU:0, one launch (start us, length us, event | category | flops | bytes accessed | tf_op | source)
XLA Modules:
  0.0 981.5 jit_solution(11105251127771665047)
XLA Ops:
  7.2 6.5 all-to-all-start
  113.2 20.2 %all-reduce.16 = (f32[8,5,64]{2,1,0:T(8,128)S(1)}, f32[8,5,64]{2,1,0:T(8,128)S(1)}) all-reduce(f32[8,5,64]{2,1,0:T(8,128)S(1)} %convolution_bitcast_fusion, f32[8,5,64]{2,1,0:T(8,128)S(1)} %convolution_bitcast_fusion.1), channel_id=1, replica_groups=mesh['wide'=4,'batch'=8] {'wide'}, use_global_device_ids=true, to_apply=%region_1.2 | all-reduce | flops 5120 | bytes 40960 | tf_op jit(solution)/shard_map/psum | solution.py:166
  145.4 3.9 all-to-all-start.2
  150.0 8.2 all-to-all-done.2
  178.0 50.7 %slice_reduce_fusion.1 = (f32[16,73216]{1,0:T(8,128)}, f32[16,73216]{1,0:T(8,128)}) fusion(f32[32,1,73216]{2,1,0:T(1,128)} %all-gather.3.cloned.1.call-done), kind=kLoop, calls=%fused_computation.7 | loop fusion | bytes 18743296 | tf_op jit(solution)/shard_map/slice | solution.py:138
  228.7 9.6 reshape.1379
  238.3 10.6 %copy.1300 = f32[286,64,64]{0,2,1:T(8,128)} copy(f32[286,64,64]{2,1,0:T(8,128)} %reshape.1379) | data formatting | bytes 9371648 | tf_op jit(solution)/shard_map/reshape | solution.py:138
  248.9 12.3 %fusion.2 = bf16[11,11,64,64]{3,1,2,0:T(8,128)(2,1)S(1)} fusion(f32[11,11,286,1]{2,1,3,0:T(8,128)S(1)} %copy-done.22, f32[286,64,64]{0,2,1:T(8,128)} %copy.1300), kind=kOutput, calls=%fused_computation.4 | convolution fusion | flops 1700954112 | bytes 5815480 | tf_op jit(solution)/shard_map/xt,tio->xio/dot_general | solution.py:137
  261.2 6.4 rev.7
  267.7 3.1 copy.1301
  270.8 4.6 convert_element_type.170
  280.6 5.1 fusion.42
  286.5 7.0 fusion.51
  300.9 7.2 fusion.54
  315.2 7.3 fusion.63
  332.7 7.4 fusion.57
  350.4 7.1 fusion.60
  360.8 9.5 reshape.1380
  370.3 10.6 %copy.1315 = f32[286,64,64]{0,2,1:T(8,128)} copy(f32[286,64,64]{2,1,0:T(8,128)} %reshape.1380) | data formatting | bytes 9371648 | tf_op jit(solution)/shard_map/reshape | solution.py:141
  380.9 12.3 %fusion = bf16[11,11,64,64]{3,1,2,0:T(8,128)(2,1)S(1)} fusion(f32[11,11,286,1]{2,1,3,0:T(8,128)S(1)} %copy-done.22, f32[286,64,64]{0,2,1:T(8,128)} %copy.1315), kind=kOutput, calls=%fused_computation.2 | convolution fusion | flops 1700954112 | bytes 5815480 | tf_op jit(solution)/shard_map/xt,tio->xio/dot_general | solution.py:140
  393.2 6.4 rev.6
  399.6 3.1 copy.1316
  402.7 4.6 convert_element_type.174
  412.5 5.1 fusion.24
  426.6 4.8 fusion.32
  435.9 5.0 fusion.36
  440.9 3.1 fusion.40
  451.8 40.2 %fusion.1575 = (f32[2,1056]{1,0:T(2,128)S(1)}, f32[2,1056,64]{1,2,0:T(8,128)S(1)}, f32[2,1056,64]{1,2,0:T(8,128)}, f32[2,1056,64]{1,2,0:T(8,128)}, f32[2,1056,64...) fusion(f32[2]{0:T(128)} %get-tuple-element.25, f32[2]{0:T(128)} %get-tuple-element.26, ...), kind=kLoop, calls=%fused_computation.2960 | loop fusion | flops 23381952 | bytes 33316240 | tf_op jit(solution)/shard_map/reduce_sum | solution.py:199
  502.1 4.2 all-to-all-start.1
  530.1 6.1 convert_reduce_fusion.5
  539.0 6.7 convert_reduce_fusion.9
  559.1 6.0 fusion.1592
  572.4 4.9 fusion.10
  579.5 4.7 fusion.1599
  585.4 5.1 fusion.14
  596.8 4.8 fusion.18
  604.5 3.2 reshape.1384
  607.7 5.8 copy.1573
  613.6 3.9 copy.1574
  617.5 7.0 fusion.1601
  624.5 12.2 %copy.1575 = f32[286,64,64]{2,1,0:T(8,128)} copy(f32[286,64,64]{0,2,1:T(8,128)} %bitcast.803) | data formatting | bytes 9371648 | tf_op jit(solution)/shard_map/xt,xio->tio/dot_general | solution.py:103
  636.6 8.8 reshape.1386
  645.5 3.2 slice_bitcast_fusion.87
  648.9 7.3 convert_reduce_fusion.8
  658.9 6.4 convert_reduce_fusion.7
  668.1 6.5 convert_reduce_fusion.6
  696.1 4.6 fusion.4
  700.7 4.7 fusion.8
  705.4 4.7 fusion.12
  710.1 4.9 fusion.16
  718.5 3.1 reshape.1381
  721.6 5.8 copy.1565
  727.5 3.7 copy.1566
  731.2 6.9 fusion.1596
  738.1 12.2 %copy.1567 = f32[286,64,64]{2,1,0:T(8,128)} copy(f32[286,64,64]{0,2,1:T(8,128)} %bitcast.802) | data formatting | bytes 9371648 | tf_op jit(solution)/shard_map/xt,xio->tio/dot_general | solution.py:100
  750.2 8.7 reshape.1383
  758.9 10.1 %pad_maximum_fusion = f32[2342912]{0:T(1024)} fusion(f32[1171456]{0:T(1024)} %reshape.1386, f32[1171456]{0:T(1024)} %reshape.1383), kind=kLoop, calls=%fused_computation | loop fusion | flops 2342912 | bytes 18743296 | tf_op jit(solution)/shard_map/concatenate | solution.py:106
  769.1 5.0 slice_bitcast_fusion.76
  774.1 6.7 slice_bitcast_fusion.54
  797.7 35.0 %fusion.48 = bf16[2,1056,64]{1,2,0:T(8,128)(2,1)S(1)} fusion(f32[1056,2,64]{0,2,1:T(8,128)} %fusion.970, s32[]{:T(128)S(6)} %select_n.3301, f32[2,1056,64]{1,2,0:T(8,128)} %get-tuple-element.164, s32[]{:T(128)S(6)} %select_n.3299, f32[2,1056,64]{1,2,0:T(8,128)} %get-tuple-element.156, s32[]{:T(128)S(6)} %select_n.3297, ...), kind=kOutput, calls=%fused_computation.57 | convolution fusion | flops 30466080 | bytes 33681388 | tf_op jit(solution)/shard_map/skc,lk->slc/dot_general | solution.py:249
  835.5 5.0 all-to-all-start.3
  842.0 40.9 %psum.31 = f32[256]{0:T(256)S(1)} all-reduce(f32[256]{0:T(256)S(1)} %pad_maximum_fusion.1), channel_id=1, replica_groups=mesh['wide'=4,'batch'=8] {'wide','batch'}, use_global_device_ids=true, to_apply=%region_29.34 | all-reduce | flops 256 | bytes 2048 | tf_op jit(solution)/shard_map/psum | solution.py:260
  887.3 75.9 %all-reduce.19.cloned.1.call-done = f32[2342912]{0:T(1024)} async-done(((f32[2342912]{0:T(1024)}), f32[2342912]{0:T(1024)}) %all-reduce.19.cloned.1.call-update) | async-done | bytes 9371664 | tf_op jit(solution)/shard_map/psum | solution.py:260
  963.2 6.0 multiply_reduce_fusion
  (1209 shorter events, 286.0 us)
Async XLA Ops:
  7.2 103.9 %copy-start.30 = (bf16[8,264,64]{1,2,0:T(8,128)(2,1)S(1)}, bf16[8,264,64]{1,2,0:T(8,128)(2,1)}, u32[]{:S(2)}) copy-start(bf16[8,264,64]{1,2,0:T(8,128)(2,1)} %param.19) | copy-start | bytes 811012
  7.2 103.9 %copy-start.367 = (s32[5]{0:T(128)S(1)}, s32[5]{0:T(128)}, u32[]{:S(2)}) copy-start(s32[5]{0:T(128)} %param.21) | copy-start | bytes 64
  7.2 104.7 %copy-start.369 = (s32[8]{0:T(128)S(1)}, s32[8]{0:T(128)}, u32[]{:S(2)}) copy-start(s32[8]{0:T(128)} %param.20) | copy-start | bytes 100
  7.2 137.5 %copy-start.353 = (f32[256]{0:T(256)S(1)}, f32[256]{0:T(256)}, u32[]{:S(2)}) copy-start(f32[256]{0:T(256)} %param.26) | copy-start | bytes 3076
  7.2 138.2 %all-to-all-start = ((bf16[8,264,64]{1,2,0:T(8,128)(2,1)}), bf16[8,264,64]{1,2,0:T(8,128)(2,1)S(1)}, u32[]{:S(2)}, u32[]{:S(2)}) async-start(bf16[8,264,64]{1,2,0:T(8,128)(2,1)} %param.19), calls=%async_computation | async-start | bytes 786432 | tf_op jit(solution)/shard_map/all_to_all | solution.py:170
  13.7 164.3 %all-gather.3.cloned.1.call-start = ((), (), s32[]{:S(2)}) async-start(), calls=%async_computation.5 | async-start | bytes 9664512 | tf_op jit(solution)/shard_map/all_gather | solution.py:135
  59.8 102.5 %copy-start.92 = (pred[1056]{0:T(1024)(128)(4,1)}, pred[1056]{0:T(1024)(128)(4,1)S(1)}, u32[]{:S(2)}) copy-start(pred[1056]{0:T(1024)(128)(4,1)S(1)} %get-tuple-element.452) | copy-start | bytes 3172
  59.8 102.6 %copy-start.89 = (pred[1056]{0:T(1024)(128)(4,1)}, pred[1056]{0:T(1024)(128)(4,1)S(1)}, u32[]{:S(2)}) copy-start(pred[1056]{0:T(1024)(128)(4,1)S(1)} %get-tuple-element.451) | copy-start | bytes 3172
  60.6 104.1 %copy-start.71 = (pred[1056]{0:T(1024)(128)(4,1)}, pred[1056]{0:T(1024)(128)(4,1)S(1)}, u32[]{:S(2)}) copy-start(pred[1056]{0:T(1024)(128)(4,1)S(1)} %get-tuple-element.446) | copy-start | bytes 3172
  60.6 104.4 %copy-start.68 = (pred[1056]{0:T(1024)(128)(4,1)}, pred[1056]{0:T(1024)(128)(4,1)S(1)}, u32[]{:S(2)}) copy-start(pred[1056]{0:T(1024)(128)(4,1)S(1)} %get-tuple-element.445) | copy-start | bytes 3172
  61.4 101.4 %copy-start.86 = (pred[1056]{0:T(1024)(128)(4,1)}, pred[1056]{0:T(1024)(128)(4,1)S(1)}, u32[]{:S(2)}) copy-start(pred[1056]{0:T(1024)(128)(4,1)S(1)} %get-tuple-element.450) | copy-start | bytes 3172
  61.4 101.8 %copy-start.80 = (pred[1056]{0:T(1024)(128)(4,1)}, pred[1056]{0:T(1024)(128)(4,1)S(1)}, u32[]{:S(2)}) copy-start(pred[1056]{0:T(1024)(128)(4,1)S(1)} %get-tuple-element.449) | copy-start | bytes 3172
  62.2 103.2 %copy-start.74 = (pred[1056]{0:T(1024)(128)(4,1)}, pred[1056]{0:T(1024)(128)(4,1)S(1)}, u32[]{:S(2)}) copy-start(pred[1056]{0:T(1024)(128)(4,1)S(1)} %get-tuple-element.444) | copy-start | bytes 3172
  62.2 104.4 %copy-start.128 = (pred[1056]{0:T(1024)(128)(4,1)}, pred[1056]{0:T(1024)(128)(4,1)S(1)}, u32[]{:S(2)}) copy-start(pred[1056]{0:T(1024)(128)(4,1)S(1)} %get-tuple-element.443) | copy-start | bytes 3172
  63.0 100.5 %copy-start.83 = (pred[1056]{0:T(1024)(128)(4,1)}, pred[1056]{0:T(1024)(128)(4,1)S(1)}, u32[]{:S(2)}) copy-start(pred[1056]{0:T(1024)(128)(4,1)S(1)} %get-tuple-element.448) | copy-start | bytes 3172
  63.0 101.3 %copy-start.77 = (pred[1056]{0:T(1024)(128)(4,1)}, pred[1056]{0:T(1024)(128)(4,1)S(1)}, u32[]{:S(2)}) copy-start(pred[1056]{0:T(1024)(128)(4,1)S(1)} %get-tuple-element.447) | copy-start | bytes 3172
  75.9 90.7 %copy-start.119 = (pred[1056]{0:T(1024)(128)(4,1)}, pred[1056]{0:T(1024)(128)(4,1)S(1)}, u32[]{:S(2)}) copy-start(pred[1056]{0:T(1024)(128)(4,1)S(1)} %get-tuple-element.433) | copy-start | bytes 3172
  91.4 75.2 %copy-start.122 = (pred[1056]{0:T(1024)(128)(4,1)}, pred[1056]{0:T(1024)(128)(4,1)S(1)}, u32[]{:S(2)}) copy-start(pred[1056]{0:T(1024)(128)(4,1)S(1)} %get-tuple-element.423) | copy-start | bytes 3172
  98.4 210.6 %copy-start.35 = (pred[1056]{0:T(1024)(128)(4,1)}, pred[1056]{0:T(1024)(128)(4,1)S(1)}, u32[]{:S(2)}) copy-start(pred[1056]{0:T(1024)(128)(4,1)S(1)} %get-tuple-element.465) | copy-start | bytes 3172
  99.2 67.4 %copy-start.125 = (pred[1056]{0:T(1024)(128)(4,1)}, pred[1056]{0:T(1024)(128)(4,1)S(1)}, u32[]{:S(2)}) copy-start(pred[1056]{0:T(1024)(128)(4,1)S(1)} %get-tuple-element.422) | copy-start | bytes 3172
  99.2 68.7 %copy-start.61 = (pred[1056]{0:T(1024)(128)(4,1)}, pred[1056]{0:T(1024)(128)(4,1)S(1)}, u32[]{:S(2)}) copy-start(pred[1056]{0:T(1024)(128)(4,1)S(1)} %get-tuple-element.421) | copy-start | bytes 3172
  100.0 68.8 %copy-start.43 = (pred[1056]{0:T(1024)(128)(4,1)}, pred[1056]{0:T(1024)(128)(4,1)S(1)}, u32[]{:S(2)}) copy-start(pred[1056]{0:T(1024)(128)(4,1)S(1)} %get-tuple-element.416) | copy-start | bytes 3172
  100.0 69.0 %copy-start.37 = (pred[1056]{0:T(1024)(128)(4,1)}, pred[1056]{0:T(1024)(128)(4,1)S(1)}, u32[]{:S(2)}) copy-start(pred[1056]{0:T(1024)(128)(4,1)S(1)} %get-tuple-element.415) | copy-start | bytes 3172
  100.8 67.2 %copy-start.58 = (pred[1056]{0:T(1024)(128)(4,1)}, pred[1056]{0:T(1024)(128)(4,1)S(1)}, u32[]{:S(2)}) copy-start(pred[1056]{0:T(1024)(128)(4,1)S(1)} %get-tuple-element.420) | copy-start | bytes 3172
  100.8 67.4 %copy-start.52 = (pred[1056]{0:T(1024)(128)(4,1)}, pred[1056]{0:T(1024)(128)(4,1)S(1)}, u32[]{:S(2)}) copy-start(pred[1056]{0:T(1024)(128)(4,1)S(1)} %get-tuple-element.419) | copy-start | bytes 3172
  101.6 67.6 %copy-start.46 = (pred[1056]{0:T(1024)(128)(4,1)}, pred[1056]{0:T(1024)(128)(4,1)S(1)}, u32[]{:S(2)}) copy-start(pred[1056]{0:T(1024)(128)(4,1)S(1)} %get-tuple-element.414) | copy-start | bytes 3172
  101.6 67.7 %copy-start.40 = (pred[1056]{0:T(1024)(128)(4,1)}, pred[1056]{0:T(1024)(128)(4,1)S(1)}, u32[]{:S(2)}) copy-start(pred[1056]{0:T(1024)(128)(4,1)S(1)} %get-tuple-element.413) | copy-start | bytes 3172
  102.4 66.0 %copy-start.55 = (pred[1056]{0:T(1024)(128)(4,1)}, pred[1056]{0:T(1024)(128)(4,1)S(1)}, u32[]{:S(2)}) copy-start(pred[1056]{0:T(1024)(128)(4,1)S(1)} %get-tuple-element.418) | copy-start | bytes 3172
  102.4 66.2 %copy-start.49 = (pred[1056]{0:T(1024)(128)(4,1)}, pred[1056]{0:T(1024)(128)(4,1)S(1)}, u32[]{:S(2)}) copy-start(pred[1056]{0:T(1024)(128)(4,1)S(1)} %get-tuple-element.417) | copy-start | bytes 3172
  133.3 26.6 %copy-start.356 = (f32[8,5,64]{2,1,0:T(8,128)}, f32[8,5,64]{2,1,0:T(8,128)S(1)}, u32[]{:S(2)}) copy-start(f32[8,5,64]{2,1,0:T(8,128)S(1)} %get-tuple-element.29) | copy-start | bytes 30724
  133.3 26.6 %copy-start.357 = (f32[8,5,64]{2,1,0:T(8,128)}, f32[8,5,64]{2,1,0:T(8,128)S(1)}, u32[]{:S(2)}) copy-start(f32[8,5,64]{2,1,0:T(8,128)S(1)} %get-tuple-element.30) | copy-start | bytes 30724
  139.3 26.1 %copy-start.116 = (pred[1056]{0:T(1024)(128)(4,1)}, pred[1056]{0:T(1024)(128)(4,1)S(1)}, u32[]{:S(2)}) copy-start(pred[1056]{0:T(1024)(128)(4,1)S(1)} %get-tuple-element.412) | copy-start | bytes 3172
  139.3 27.3 %copy-start.131 = (pred[1056]{0:T(1024)(128)(4,1)}, pred[1056]{0:T(1024)(128)(4,1)S(1)}, u32[]{:S(2)}) copy-start(pred[1056]{0:T(1024)(128)(4,1)S(1)} %get-tuple-element.411) | copy-start | bytes 3172
  140.1 34.4 %copy-start.98 = (pred[1056]{0:T(1024)(128)(4,1)}, pred[1056]{0:T(1024)(128)(4,1)S(1)}, u32[]{:S(2)}) copy-start(pred[1056]{0:T(1024)(128)(4,1)S(1)} %get-tuple-element.406) | copy-start | bytes 3172
  140.1 35.3 %copy-start.95 = (pred[1056]{0:T(1024)(128)(4,1)}, pred[1056]{0:T(1024)(128)(4,1)S(1)}, u32[]{:S(2)}) copy-start(pred[1056]{0:T(1024)(128)(4,1)S(1)} %get-tuple-element.405) | copy-start | bytes 3172
  140.9 28.4 %copy-start.113 = (pred[1056]{0:T(1024)(128)(4,1)}, pred[1056]{0:T(1024)(128)(4,1)S(1)}, u32[]{:S(2)}) copy-start(pred[1056]{0:T(1024)(128)(4,1)S(1)} %get-tuple-element.410) | copy-start | bytes 3172
  140.9 29.9 %copy-start.107 = (pred[1056]{0:T(1024)(128)(4,1)}, pred[1056]{0:T(1024)(128)(4,1)S(1)}, u32[]{:S(2)}) copy-start(pred[1056]{0:T(1024)(128)(4,1)S(1)} %get-tuple-element.409) | copy-start | bytes 3172
  141.7 34.6 %copy-start.101 = (pred[1056]{0:T(1024)(128)(4,1)}, pred[1056]{0:T(1024)(128)(4,1)S(1)}, u32[]{:S(2)}) copy-start(pred[1056]{0:T(1024)(128)(4,1)S(1)} %get-tuple-element.404) | copy-start | bytes 3172
  141.7 35.5 %copy-start.64 = (pred[1056]{0:T(1024)(128)(4,1)}, pred[1056]{0:T(1024)(128)(4,1)S(1)}, u32[]{:S(2)}) copy-start(pred[1056]{0:T(1024)(128)(4,1)S(1)} %get-tuple-element.403) | copy-start | bytes 3172
  142.5 29.5 %copy-start.110 = (pred[1056]{0:T(1024)(128)(4,1)}, pred[1056]{0:T(1024)(128)(4,1)S(1)}, u32[]{:S(2)}) copy-start(pred[1056]{0:T(1024)(128)(4,1)S(1)} %get-tuple-element.408) | copy-start | bytes 3172
  142.5 31.1 %copy-start.104 = (pred[1056]{0:T(1024)(128)(4,1)}, pred[1056]{0:T(1024)(128)(4,1)S(1)}, u32[]{:S(2)}) copy-start(pred[1056]{0:T(1024)(128)(4,1)S(1)} %get-tuple-element.407) | copy-start | bytes 3172
  145.3 16.2 %copy-start.355 = (f32[64]{0:T(128)}, f32[64]{0:T(128)S(1)}, u32[]{:S(2)}) copy-start(f32[64]{0:T(128)S(1)} %get-tuple-element.394) | copy-start | bytes 772
  145.4 12.8 %all-to-all-start.2 = ((bf16[8,264,64]{1,2,0:T(8,128)(2,1)}), bf16[8,264,64]{1,2,0:T(8,128)(2,1)S(1)}, u32[]{:S(2)}, u32[]{:S(2)}) async-start(bf16[8,264,64]{1,2,0:T(8,128)(2,1)} %param.22), calls=%async_computation.2 | async-start | bytes 786432 | tf_op jit(solution)/shard_map/all_to_all | solution.py:171
  149.4 344.5 %copy-start.33 = (pred[2,1056]{1,0:T(4,128)(4,1)}, pred[2,1056]{1,0:T(4,128)(4,1)S(1)}, u32[]{:S(2)}) copy-start(pred[2,1056]{1,0:T(4,128)(4,1)S(1)} %iota_compare_fusion) | copy-start | bytes 6340
  451.8 40.5 %copy-start.8 = (f32[2,1056,64]{1,2,0:T(8,128)S(1)}, f32[2,1056,64]{1,2,0:T(8,128)}, u32[]{:S(2)}) copy-start(f32[2,1056,64]{1,2,0:T(8,128)} %reshape.1387) | copy-start | bytes 1622020
  451.8 42.1 %copy-start.134 = (f32[2,1056]{1,0:T(2,128)S(1)}, f32[2,1056]{1,0:T(2,128)}, u32[]{:S(2)}) copy-start(f32[2,1056]{1,0:T(2,128)} %div.83) | copy-start | bytes 25348
  496.5 12.6 %copy-start.349 = (pred[1056]{0:T(1024)(128)(4,1)S(1)}, pred[1056]{0:T(1024)(128)(4,1)}, u32[]{:S(2)}) copy-start(pred[1056]{0:T(1024)(128)(4,1)} %get-tuple-element.507) | copy-start | bytes 3172
  496.5 12.9 %copy-start.348 = (pred[1056]{0:T(1024)(128)(4,1)S(1)}, pred[1056]{0:T(1024)(128)(4,1)}, u32[]{:S(2)}) copy-start(pred[1056]{0:T(1024)(128)(4,1)} %get-tuple-element.508) | copy-start | bytes 3172
  496.5 13.2 %copy-start.351 = (pred[1056]{0:T(1024)(128)(4,1)S(1)}, pred[1056]{0:T(1024)(128)(4,1)}, u32[]{:S(2)}) copy-start(pred[1056]{0:T(1024)(128)(4,1)} %get-tuple-element.509) | copy-start | bytes 3172
  497.9 12.6 %copy-start.352 = (pred[1056]{0:T(1024)(128)(4,1)S(1)}, pred[1056]{0:T(1024)(128)(4,1)}, u32[]{:S(2)}) copy-start(pred[1056]{0:T(1024)(128)(4,1)} %get-tuple-element.511) | copy-start | bytes 3172
  497.9 13.0 %copy-start.339 = (pred[1056]{0:T(1024)(128)(4,1)S(1)}, pred[1056]{0:T(1024)(128)(4,1)}, u32[]{:S(2)}) copy-start(pred[1056]{0:T(1024)(128)(4,1)} %get-tuple-element.547) | copy-start | bytes 3172
  497.9 13.3 %copy-start.338 = (pred[1056]{0:T(1024)(128)(4,1)S(1)}, pred[1056]{0:T(1024)(128)(4,1)}, u32[]{:S(2)}) copy-start(pred[1056]{0:T(1024)(128)(4,1)} %get-tuple-element.548) | copy-start | bytes 3172
  502.1 333.4 %all-to-all-start.1 = ((bf16[4,2,16896]{2,1,0:T(2,128)(2,1)}), bf16[4,2,16896]{2,1,0:T(2,128)(2,1)}, u32[]{:S(2)}, u32[]{:S(2)}) async-start(bf16[4,2,16896]{2,1,0:T(2,128)(2,1)} %reshape.1450), calls=%async_computation.1 | async-start | bytes 540672 | tf_op jit(solution)/shard_map/all_to_all | solution.py:253
  506.3 456.9 %all-reduce.19.cloned.1.call-start = ((), (), s32[]{:S(2)}) async-start(), calls=%async_computation.4 | async-start | bytes 18743296 | tf_op jit(solution)/shard_map/psum | solution.py:260
  545.7 20.2 %copy-start = (bf16[2,1056,64]{1,2,0:T(8,128)(2,1)}, bf16[2,1056,64]{1,2,0:T(8,128)(2,1)S(1)}, u32[]{:S(2)}) copy-start(bf16[2,1056,64]{1,2,0:T(8,128)(2,1)S(1)} %get-tuple-element.40) | copy-start | bytes 811012
  636.6 21.2 %slice-start.2 = ((s8[6488064]{0:T(1024)(128)(4,1)}), s8[2293760]{0:T(1024)(128)(4,1)S(1)}, s32[]{:S(2)}) async-start(s8[6488064]{0:T(1024)(128)(4,1)} %bitcast.814), calls=%async_computation.8 | async-start | bytes 4587520
  645.5 12.3 %slice-start.3 = ((s8[6488064]{0:T(1024)(128)(4,1)}), s8[4194304]{0:T(1024)(128)(4,1)S(1)}, s32[]{:S(2)}) async-start(s8[6488064]{0:T(1024)(128)(4,1)} %bitcast.814), calls=%async_computation.9 | async-start | bytes 8388608
  835.5 50.3 %all-to-all-start.3 = ((bf16[4,2,16896]{2,1,0:T(2,128)(2,1)}), bf16[4,2,16896]{2,1,0:T(2,128)(2,1)S(1)}, u32[]{:S(2)}, u32[]{:S(2)}) async-start(bf16[4,2,16896]{2,1,0:T(2,128)(2,1)} %reshape.1452), calls=%async_computation.3 | async-start | bytes 540672 | tf_op jit(solution)/shard_map/all_to_all | solution.py:254
  887.3 83.3 %copy-start.354 = (f32[256]{0:T(256)S(1)}, f32[256]{0:T(256)}, u32[]{:S(2)}) copy-start(f32[256]{0:T(256)} %param.26) | copy-start | bytes 3076
  887.3 83.3 %copy-start.365 = (f32[256]{0:T(256)S(1)}, f32[256]{0:T(256)}, u32[]{:S(2)}) copy-start(f32[256]{0:T(256)} %param.27) | copy-start | bytes 3076
  887.3 83.3 %copy-start.366 = (f32[256]{0:T(256)S(1)}, f32[256]{0:T(256)}, u32[]{:S(2)}) copy-start(f32[256]{0:T(256)} %param.28) | copy-start | bytes 3076
  887.3 83.9 %copy-start.21 = (f32[73216]{0:T(1024)S(1)}, f32[73216]{0:T(1024)}, u32[]{:S(2)}) copy-start(f32[73216]{0:T(1024)} %param.23) | copy-start | bytes 878596
  887.3 83.9 %copy-start.31 = (f32[73216]{0:T(1024)S(1)}, f32[73216]{0:T(1024)}, u32[]{:S(2)}) copy-start(f32[73216]{0:T(1024)} %param.24) | copy-start | bytes 878596
  887.3 83.9 %copy-start.32 = (f32[73216]{0:T(1024)S(1)}, f32[73216]{0:T(1024)}, u32[]{:S(2)}) copy-start(f32[73216]{0:T(1024)} %param.25) | copy-start | bytes 878596
  (321 other events, 1146.4 us)
Sparse Core Ops, SparseCore 0:
  18.0 83.1 all-gather.2
  769.2 193.9 all-reduce.18
where the time goes:
time: 991 us; the launch traced here: 982 us
  other arithmetic  286 us (29%)
  local copies, waits for them, and re-layouts  277 us (28%)
  matrix products  191 us (19%)
  waiting for transfers between devices  84.1 us (8%)
  between operations  63 us (6%)
  blocking collectives  61 us (6%)
  starting transfers between devices  20 us (2%)
    dot_general x20, matrix products, conv_apply(): jnp.einsum('slk,km->slm', shifted, matrix, preferred_element_type=jnp.flo...  79.6 us
    psum x1, waiting for transfers between devices, local(): full_grad, small_sum = lax.psum((flat_grad, small_grad), ('wide', 'batch'))  75.9 us
    unnamed x244, other arithmetic  70.9 us
    slice x1, local copies, waits for them, and re-layouts, local(): whole_kernels[:split_at].reshape(TAPS, C, FF)  50.7 us
    psum x1, blocking collectives, local(): full_grad, small_sum = lax.psum((flat_grad, small_grad), ('wide', 'batch'))  40.9 us
    squeeze x20, local copies, waits for them, and re-layouts, rows_sum(): spread[:, :, row_off + HALF, :]  40.6 us
    reduce_sum x1, other arithmetic, local(): centered = merged - jnp.mean(merged, axis=2, keepdims=True)  40.2 us
    convert_element_type x5, other arithmetic, local(): activated = jax.nn.gelu(hidden_pre, approximate=False).astype(jnp.bfloat16)  36 us
  transfers between devices with their start and end apart: 6, of which 2 were waited for; matrix products, arithmetic and copies ran while one was open for 42% of the time, Pallas kernels for 0%

commit v1 on v0

v1 whole, which is shorter than its diff:
```python
import functools
import math

import jax
import jax.numpy as jnp
import numpy as np
from jax import lax
from jax.experimental import pallas as pl
from jax.experimental.pallas import tpu as pltpu
from jax.sharding import PartitionSpec as P

C = 64
K = 5
NKER = 6
STEP = 10
SPAN = 11
HALF = 5
TAPS = 286
CELLS = SPAN * SPAN
TAP = C * C

beta_one = 0.9
beta_two = 0.999
learn_rate = 0.1
weight_decay = 0.01
adam_eps = 1e-08
clip_norm = 1.0
norm_eps = 1e-05
inv_root_two = 1.0 / math.sqrt(2.0)
inv_root_tau = 1.0 / math.sqrt(2.0 * math.pi)

bf16 = jnp.bfloat16
f32 = jnp.float32
precise = lax.Precision.HIGHEST

OFFS = (-1, 0, 1, 2, -3, -2, 3, 4, -5, -4, 5, 6)
BASES = (-1, 1, -3, 3, -5, 5)
W = 12 * C
CH = 96


def tap_cells():
    cells = []
    for block in range(2):
        for kernel in range(NKER):
            for row_off in range(-kernel, kernel + 1):
                for col_off in range(-kernel, kernel + 1):
                    cells.append(block * CELLS + (row_off + HALF) * SPAN + col_off + HALF)
    return np.array(cells)


@functools.lru_cache(None)
def plan(count):
    cells = tap_cells()
    share = cells.size * TAP // count
    span = max((share * (d + 1) - 1) // TAP - share * d // TAP + 1 for d in range(count))
    needs = []
    clash = [set() for _ in range(2 * CELLS)]
    for d in range(count):
        first = share * d // TAP
        last = (share * (d + 1) - 1) // TAP
        need = set(cells[first : last + 1].tolist())
        needs.append((first, last, need))
        for cell in need:
            clash[cell].update(need)
    room = -(-2 * CELLS // count)
    order = sorted(range(2 * CELLS), key=lambda cell: -len(clash[cell]))
    for seed in range(1000):
        rng = np.random.RandomState(seed)
        owner = np.full(2 * CELLS, -1)
        filled = np.zeros(count, int)
        for cell in order:
            used = {owner[other] for other in clash[cell]}
            free = [d for d in range(count) if d not in used and filled[d] < room]
            if not free:
                break
            least = min(filled[d] for d in free)
            free = [d for d in free if filled[d] == least]
            owner[cell] = free[rng.randint(len(free))]
            filled[owner[cell]] += 1
        else:
            break
    place = np.zeros(2 * CELLS, int)
    filled[:] = 0
    for cell in range(2 * CELLS):
        place[cell] = filled[owner[cell]]
        filled[owner[cell]] += 1
    spread = np.zeros((count, count, span), np.float32)
    pick = np.zeros((count, room, count), np.float32)
    for d, (first, last, need) in enumerate(needs):
        for tap in range(first, last + 1):
            spread[d, owner[cells[tap]], tap - first] = 1.0
        for cell in need:
            pick[owner[cell], place[cell], d] = 1.0
    weight = np.zeros((count, room), np.float32)
    for cell in range(2 * CELLS):
        row, col = divmod(cell % CELLS, SPAN)
        weight[owner[cell], place[cell]] = NKER - max(abs(row - HALF), abs(col - HALF))
    row_of = owner * room + place
    return span, room, spread, pick, weight, row_of


def block_kernel(
    length,
    freq_ref,
    len_ref,
    x_ref,
    cot_ref,
    trig_ref,
    w1_ref,
    w2_ref,
    small_ref,
    out_ref,
    gser_ref,
    gm1_ref,
    gm2_ref,
    gsm_ref,
    xf_ref,
    af_ref,
    pk_ref,
    xs_ref,
    s_ref,
    gf_ref,
    gp_ref,
    gr_ref,
    act_ref,
    slope_ref,
    br_ref,
    mg_ref,
    gin_ref,
    wi_ref,
    w1s_ref,
    w2s_ref,
    w1r_ref,
    w2r_ref,
    wv_ref,
    gw_ref,
    gb_ref,
):
    L = length
    NCH = L // CH
    GP = 544

    def lanes(rows):
        return lax.broadcasted_iota(jnp.int32, (rows, 128), 1) < C

    def swap(v):
        return pltpu.roll(v, C, 1)

    def rows(i, n=CH):
        return pl.ds(pl.multiple_of(i * n, 16), n)

    def half_sum(v):
        low = lanes(v.shape[0])
        a = jnp.sum(jnp.where(low, v, 0.0), axis=1, keepdims=True)
        b = jnp.sum(jnp.where(low, 0.0, v), axis=1, keepdims=True)
        return jnp.where(low, a, b)

    def fold(v):
        return jnp.sum(v.reshape(v.shape[0] // 8, 8, 128), axis=0)

    def period(j):
        return L // freq_ref[j]

    s_zero = jnp.zeros((CH, 128), f32)
    for b in range(11):

        @pl.loop(0, NCH)
        def _(i):
            s_ref[b, rows(i), :] = s_zero
            s_ref[b, pl.ds(pl.multiple_of(2 * L + i * CH, 16), CH), :] = s_zero

    for s in range(2):
        for start, stop in ((0, L), (L + 1632, gf_ref.shape[1])):

            @pl.loop(0, (stop - start) // 16)
            def _(i):
                gf_ref[s, pl.ds(pl.multiple_of(start + i * 16, 8), 16), :] = jnp.zeros((16, 128), f32)

    for start, stop in ((0, GP), (GP + L, gp_ref.shape[0])):

        @pl.loop(0, (stop - start) // 16)
        def _(i):
            gp_ref[pl.ds(pl.multiple_of(start + i * 16, 8), 16), :] = jnp.zeros((16, 128), f32)

    pk_ref[0:16, :] = jnp.zeros((16, 128), f32)
    pk_ref[L + 16 : L + 48, :] = jnp.zeros((32, 128), f32)

    for src, cols, rws in ((w1_ref, w1s_ref, w1r_ref), (w2_ref, w2s_ref, w2r_ref)):
        for q in range(6):
            cols[:, 128 * q : 128 * q + 128] = swap(
                src[:, 128 * q : 128 * q + 128].astype(f32)
            ).astype(bf16)
            rws[128 * q : 128 * q + 64, :] = src[128 * q + 64 : 128 * q + 128, :]
            rws[128 * q + 64 : 128 * q + 128, :] = src[128 * q : 128 * q + 64, :]

    gm1_ref[...] = jnp.zeros((W, W), f32)
    gm2_ref[...] = jnp.zeros((W, W), f32)
    gb_ref[...] = jnp.zeros((4, 8, 128), f32)
    gw_ref[...] = jnp.zeros((K, 8, 128), f32)

    own = jnp.where(lanes(1), len_ref[0], len_ref[1])

    def valid(i, n=CH):
        return i * n + lax.broadcasted_iota(jnp.int32, (n, 128), 0) < own

    @pl.loop(0, NCH)
    def _(i):
        v = jnp.where(valid(i), x_ref[rows(i), :].astype(f32), 0.0)
        mg_ref[rows(i), :] = v
        pk_ref[pl.ds(pl.multiple_of(16 + i * CH, 16), CH), :] = v

    def fill_pairs(dst):
        def step(t0, n):
            a = pk_ref[pl.ds(16 + t0, n), :]
            b = pk_ref[pl.ds(17 + t0, n), :]
            low = lanes(n)
            dst[0, pl.ds(8 + t0, n), :] = jnp.where(low, a, swap(b))
            dst[1, pl.ds(8 + t0, n), :] = jnp.where(low, swap(a), b)

        @pl.loop(0, NCH)
        def _(i):
            step(pl.multiple_of(i * CH, 8) - 8, CH)

        step(L - 8, 16)

    fill_pairs(xf_ref)

    xm = mg_ref[...].astype(bf16)
    spec = lax.dot_general(
        trig_ref[...], xm, (((0,), (0,)), ((), ())), preferred_element_type=f32
    )
    spec = (spec[0:16] + spec[16:32] + spec[32:48]) * (2.0 / L)
    real, imag = spec[0:8], spec[8:16]
    magnitude = jnp.sqrt(real * real + imag * imag + 1.0)
    mean_mag = half_sum(magnitude) * (1.0 / C)
    live = lax.broadcasted_iota(jnp.int32, (8, 128), 0) < K
    top = jnp.max(jnp.where(live, mean_mag, -1e30), axis=0, keepdims=True)
    ex = jnp.where(live, jnp.exp(mean_mag - top), 0.0)
    weights = ex / jnp.sum(ex, axis=0, keepdims=True)
    wv_ref[...] = weights

    def fill_within(p):
        inv = 1.0 / jnp.full((CH, 128), p, jnp.int32).astype(f32)
        high = jnp.where(lanes(CH), 0, 1)

        @pl.loop(0, NCH)
        def _(i):
            t = i * CH + lax.broadcasted_iota(jnp.int32, (CH, 128), 0)
            q = ((t.astype(f32) + 0.5) * inv).astype(jnp.int32)
            wi_ref[rows(i), :] = t - q * p + high

    def build_cols(src, p, nk):
        @pl.loop(0, NCH)
        def _(i):
            wi = wi_ref[rows(i), :]
            for q in range(2 * nk):
                base = BASES[q]
                keep = wi >= -base if base < 0 else wi < p - base
                for s in range(2):
                    v = src[s, pl.ds(8 + base + i * CH, CH), :]
                    xs_ref[pl.ds(pl.multiple_of(s * L + i * CH, 16), CH), 128 * q : 128 * q + 128] = (
                        jnp.where(keep, v, 0.0).astype(bf16)
                    )

    RM = L

    def to_slots(get, tiles):
        low = lanes(RM)
        for n in range(tiles):
            d0, d1 = get(n)
            for h in range(2):
                a = d0[:, 128 * h : 128 * h + 128]
                b = d1[:, 128 * h : 128 * h + 128]
                s_ref[4 * n + 2 * h, L : 2 * L, :] = jnp.where(low, a, b)
                if 4 * n + 2 * h + 1 < 11:
                    s_ref[4 * n + 2 * h + 1, L : 2 * L, :] = jnp.where(low, b, a)

    def mm_forward(w_ref, ws_ref, nk, nr):
        def get(n):
            cut = slice(256 * n, 256 * n + 256)
            return (
                jnp.dot(xs_ref[0:L, : 256 * nk], w_ref[: 256 * nk, cut], preferred_element_type=f32),
                jnp.dot(
                    xs_ref[L : 2 * L, : 256 * nk], ws_ref[: 256 * nk, cut], preferred_element_type=f32
                ),
            )

        to_slots(get, nr)

    def mm_adjoint(w_ref, wr_ref, nk, nr):
        dims = (((1,), (1,)), ((), ()))

        def get(n):
            cut = slice(256 * n, 256 * n + 256)
            return (
                lax.dot_general(
                    gr_ref[0:L, : 256 * nr], w_ref[cut, : 256 * nr], dims, preferred_element_type=f32
                ),
                lax.dot_general(
                    gr_ref[L : 2 * L, : 256 * nr],
                    wr_ref[cut, : 256 * nr],
                    dims,
                    preferred_element_type=f32,
                ),
            )

        to_slots(get, nk)

    def mm_weights(gm_ref, nk, nr):
        for n in range(nr):
            cut = slice(256 * n, 256 * n + 256)
            gm_ref[: 256 * nk, cut] += lax.dot_general(
                xs_ref[:, : 256 * nk],
                gr_ref[:, cut],
                (((0,), (0,)), ((), ())),
                preferred_element_type=f32,
            )

    def sum_rows(i, p, nr):
        even = jnp.zeros((CH, 128), f32)
        odd = even
        for b in range(min(4 * nr, 11)):
            off = L + jnp.clip(OFFS[b] * p, -L, L)
            v = s_ref[b, pl.ds(off + i * CH, CH), :]
            if b % 2 == 0:
                even = even + v
            else:
                odd = odd + v
        return even + swap(odd)

    def sum_cols(i, p, nk):
        wi = wi_ref[rows(i), :] - jnp.where(lanes(CH), 0, 1)
        even = jnp.zeros((CH, 128), f32)
        odd = even
        for b in range(min(4 * nk, 11)):
            d = OFFS[b]
            v = s_ref[b, pl.ds(L - d + i * CH, CH), :]
            if d < 0:
                v = jnp.where(wi < p + d, v, 0.0)
            elif d > 0:
                v = jnp.where(wi >= d, v, 0.0)
            if b % 2 == 0:
                even = even + v
            else:
                odd = odd + v
        return even + swap(odd)

    def build_rows(p, nr):
        @pl.loop(0, 17)
        def _(i):
            a = gp_ref[pl.ds(pl.multiple_of(GP + i * CH, 8), CH), :]
            b = gp_ref[pl.ds(GP - p + i * CH, CH), :]
            low = lanes(CH)
            at = pl.ds(pl.multiple_of(L + i * CH, 8), CH)
            gf_ref[0, at, :] = jnp.where(low, a, swap(b))
            gf_ref[1, at, :] = jnp.where(low, swap(a), b)

        @pl.loop(0, NCH)
        def _(i):
            for q in range(2 * nr):
                off = L + jnp.clip(-BASES[q] * p, -L, L + p)
                for s in range(2):
                    v = gf_ref[s, pl.ds(off + i * CH, CH), :]
                    gr_ref[pl.ds(pl.multiple_of(s * L + i * CH, 16), CH), 128 * q : 128 * q + 128] = (
                        v.astype(bf16)
                    )

    def forward(j, nk, nr):
        p = period(j)
        fill_within(p)
        build_cols(xf_ref, p, nk)
        mm_forward(w1_ref, w1s_ref, nk, nr)
        bias_one = small_ref[0:1, :]
        bias_two = small_ref[1:2, :]

        @pl.loop(0, NCH)
        def _(i):
            h = sum_rows(i, p, nr) + bias_one
            cdf = 0.5 * (1.0 + lax.erf(h * inv_root_two))
            act = (h * cdf).astype(bf16)
            slope_ref[j, rows(i), :] = cdf + h * jnp.exp(-0.5 * h * h) * inv_root_tau
            act_ref[j, rows(i), :] = act
            pk_ref[pl.ds(pl.multiple_of(16 + i * CH, 16), CH), :] = act.astype(f32)

        fill_pairs(af_ref)
        build_cols(af_ref, p, nk)
        mm_forward(w2_ref, w2s_ref, nk, nr)
        wj = wv_ref[pl.ds(j, 1), :]

        @pl.loop(0, NCH)
        def _(i):
            v = sum_rows(i, p, nr) + bias_two
            br_ref[j, rows(i), :] = v
            mg_ref[rows(i), :] += wj * v

    forward(0, 3, 1)

    @pl.loop(1, K - 1)
    def _(j):
        forward(j, 3, 3)

    forward(K - 1, 1, 3)

    same = (
        lax.broadcasted_iota(jnp.int32, (384, 128), 0) % 128 // C
        == lax.broadcasted_iota(jnp.int32, (384, 128), 1) // C
    )
    ones = jnp.where(same, 1.0 / C, 0.0).astype(bf16)

    def half_mean(v):
        a = v.astype(bf16)
        r = v - a.astype(f32)
        b = r.astype(bf16)
        c = (r - b.astype(f32)).astype(bf16)
        return jnp.dot(jnp.concatenate([a, b, c], axis=1), ones, preferred_element_type=f32)

    gain = small_ref[2:3, :]
    shift = small_ref[3:4, :]
    NB = 352

    @pl.loop(0, L // NB)
    def _(i):
        m = mg_ref[rows(i, NB), :]
        ok = valid(i, NB)
        centered = m - half_mean(m)
        inverse = lax.rsqrt(half_mean(centered * centered) + norm_eps)
        normed = centered * inverse
        out_ref[rows(i, NB), :] = jnp.where(ok, normed * gain + shift, 0.0).astype(bf16)
        g_out = jnp.where(ok, cot_ref[rows(i, NB), :].astype(f32), 0.0)
        gb_ref[2] += fold(g_out * normed)
        gb_ref[3] += fold(g_out)
        g_norm = g_out * gain
        gm = inverse * (g_norm - half_mean(g_norm) - normed * half_mean(g_norm * normed))
        mg_ref[rows(i, NB), :] = gm
        gin_ref[rows(i, NB), :] = gm

    def backward(j, nk, nr):
        p = period(j)
        fill_within(p)
        wj = wv_ref[pl.ds(j, 1), :]

        @pl.loop(0, NCH)
        def _(i):
            gm = mg_ref[rows(i), :]
            gw_ref[j] += fold(gm * br_ref[j, rows(i), :])
            g = (wj * gm).astype(bf16).astype(f32)
            gb_ref[1] += fold(g)
            gp_ref[pl.ds(pl.multiple_of(GP + i * CH, 8), CH), :] = g
            pk_ref[pl.ds(pl.multiple_of(16 + i * CH, 16), CH), :] = act_ref[j, rows(i), :].astype(f32)

        build_rows(p, nr)
        mm_adjoint(w2_ref, w2r_ref, nk, nr)
        fill_pairs(af_ref)
        build_cols(af_ref, p, nk)
        mm_weights(gm2_ref, nk, nr)

        @pl.loop(0, NCH)
        def _(i):
            g = (sum_cols(i, p, nk) * slope_ref[j, rows(i), :]).astype(bf16).astype(f32)
            gb_ref[0] += fold(g)
            gp_ref[pl.ds(pl.multiple_of(GP + i * CH, 8), CH), :] = g

        build_rows(p, nr)
        mm_adjoint(w1_ref, w1r_ref, nk, nr)
        build_cols(xf_ref, p, nk)
        mm_weights(gm1_ref, nk, nr)

        @pl.loop(0, NCH)
        def _(i):
            gin_ref[rows(i), :] += sum_cols(i, p, nk)

    backward(0, 3, 1)

    @pl.loop(1, K - 1)
    def _(j):
        backward(j, 3, 3)

    backward(K - 1, 1, 3)

    row8 = lax.broadcasted_iota(jnp.int32, (8, 128), 0)
    g_weights = jnp.zeros((8, 128), f32)
    for j in range(K):
        total = jnp.sum(gw_ref[j], axis=0, keepdims=True)
        g_weights = jnp.where(row8 == j, total, g_weights)
    g_weights = half_sum(g_weights)
    weights = wv_ref[...]
    g_score = weights * (g_weights - jnp.sum(weights * g_weights, axis=0, keepdims=True))
    coeff = g_score / (magnitude * C) * (2.0 / L)
    coef = jnp.concatenate([coeff * real, coeff * imag], axis=0)
    c_hi = coef.astype(bf16)
    c_lo = (coef - c_hi.astype(f32)).astype(bf16)
    c_all = jnp.concatenate([c_hi, c_hi, c_hi], axis=0)

    @pl.loop(0, L // NB)
    def _(i):
        t = trig_ref[rows(i, NB), :]
        g = (
            gin_ref[rows(i, NB), :]
            + jnp.dot(t, c_all, preferred_element_type=f32)
            + jnp.dot(t[:, 0:16], c_lo, preferred_element_type=f32)
        )
        gser_ref[rows(i, NB), :] = jnp.where(valid(i, NB), g, 0.0).astype(bf16)

    for q in range(4):
        total = jnp.sum(gb_ref[q], axis=0, keepdims=True)
        gsm_ref[q : q + 1, :] = total + swap(total)


def run_block(x, cot, lens, freqs, w1, w2, small):
    L = x.shape[0]
    positions = jnp.arange(L, dtype=jnp.int32)
    turns = positions[:, None] * freqs[None, :] % L
    angle = turns.astype(f32) * (2.0 * math.pi / L)
    pad = ((0, 0), (0, 8 - K))
    trig = jnp.concatenate([jnp.pad(jnp.cos(angle), pad), jnp.pad(jnp.sin(angle), pad)], axis=1)
    hi = lax.reduce_precision(trig, 8, 7)
    rest = trig - hi
    mid = lax.reduce_precision(rest, 8, 7)
    trig = jnp.concatenate([hi, mid, rest - mid], axis=1).astype(bf16)
    packed = small.reshape(4, C)
    packed = jnp.concatenate([packed, packed], axis=1)
    vm = pl.BlockSpec(memory_space=pltpu.VMEM)
    sm = pl.BlockSpec(memory_space=pltpu.SMEM)
    sds = jax.ShapeDtypeStruct
    out, gser, gm1, gm2, gsm = pl.pallas_call(
        functools.partial(block_kernel, L),
        out_shape=(
            sds((L, 128), bf16),
            sds((L, 128), bf16),
            sds((W, W), f32),
            sds((W, W), f32),
            sds((4, 128), f32),
        ),
        in_specs=[sm, sm, vm, vm, vm, vm, vm, vm],
        out_specs=(vm,) * 5,
        scratch_shapes=[
            pltpu.VMEM((2, L + 16, 128), f32),
            pltpu.VMEM((2, L + 16, 128), f32),
            pltpu.VMEM((L + 48, 128), f32),
            pltpu.VMEM((2 * L, W), bf16),
            pltpu.VMEM((11, 3 * L, 128), f32),
            pltpu.VMEM((2, 3552, 128), f32),
            pltpu.VMEM((544 + L + 576, 128), f32),
            pltpu.VMEM((2 * L, W), bf16),
            pltpu.VMEM((K, L, 128), bf16),
            pltpu.VMEM((K, L, 128), f32),
            pltpu.VMEM((K, L, 128), f32),
            pltpu.VMEM((L, 128), f32),
            pltpu.VMEM((L, 128), f32),
            pltpu.VMEM((L, 128), jnp.int32),
            pltpu.VMEM((W, W), bf16),
            pltpu.VMEM((W, W), bf16),
            pltpu.VMEM((W, W), bf16),
            pltpu.VMEM((W, W), bf16),
            pltpu.VMEM((8, 128), f32),
            pltpu.VMEM((K, 8, 128), f32),
            pltpu.VMEM((4, 8, 128), f32),
        ],
        compiler_params=pltpu.CompilerParams(vmem_limit_bytes=60 << 20),
        name="block",
    )(freqs, lens, x, cot, trig, w1, w2, packed)
    return out, gser, gm1, gm2, gsm[:, :C].reshape(-1)


def adam_update(param, grad, first, second):
    first_new = beta_one * first + (1.0 - beta_one) * grad
    second_new = beta_two * second + (1.0 - beta_two) * grad * grad
    first_hat = first_new / (1.0 - beta_one**STEP)
    second_hat = second_new / (1.0 - beta_two**STEP)
    param_new = param - learn_rate * (
        first_hat / (jnp.sqrt(second_hat) + adam_eps) + weight_decay * param
    )
    return (param_new, first_new, second_new)


SLOT_OF = np.argsort(OFFS[:11])
CELL_OF = [off + HALF for off in OFFS[:11]]


def to_matrix(merged):
    grid = merged.reshape(SPAN, SPAN, C, C)
    grid = jnp.concatenate([grid[o : o + 1] for o in CELL_OF], axis=0)
    grid = jnp.concatenate([grid[:, o : o + 1] for o in CELL_OF], axis=1)
    mat = grid.transpose(1, 2, 0, 3).reshape(SPAN * C, SPAN * C)
    return jnp.pad(mat, ((0, C), (0, C)))


def from_matrix(mat):
    grid = mat[: SPAN * C, : SPAN * C].reshape(SPAN, C, SPAN, C).transpose(2, 0, 1, 3)
    grid = jnp.concatenate([grid[o : o + 1] for o in SLOT_OF], axis=0)
    grid = jnp.concatenate([grid[:, o : o + 1] for o in SLOT_OF], axis=1)
    return grid.reshape(CELLS, TAP)


def local(series, lengths, freqs, cotangent, kernels, kernel_m, kernel_v, small, small_m, small_v):
    wide_count = lax.axis_size("wide")
    count = wide_count * lax.axis_size("batch")
    wide_index = lax.axis_index("wide")
    me = lax.axis_index(("wide", "batch"))
    both = ("wide", "batch")
    span, room, spread, pick, weight, row_of = plan(count)
    share = kernels.shape[0]

    spread_me = lax.dynamic_index_in_dim(jnp.asarray(spread), me, 0, keepdims=False)
    pick_me = lax.dynamic_index_in_dim(jnp.asarray(pick), me, 0, keepdims=False)
    weight_me = lax.dynamic_index_in_dim(jnp.asarray(weight), me, 0, keepdims=False)
    lead = me * share % TAP
    taps = lax.dynamic_update_slice_in_dim(jnp.zeros((span * TAP,), f32), kernels, lead, 0)
    slots = jnp.einsum("ot,tw->ow", spread_me, taps.reshape(span, TAP), precision=precise)
    got = lax.all_to_all(slots, both, split_axis=0, concat_axis=0, tiled=True)
    merged = jnp.einsum("kd,dw->kw", pick_me, got, precision=precise) * (1.0 / NKER)
    merged = lax.all_gather(merged.astype(bf16), both, axis=0, tiled=True)
    merged = jnp.take(merged, jnp.asarray(row_of), axis=0)
    w1 = to_matrix(merged[:CELLS])
    w2 = to_matrix(merged[CELLS:])

    local_series = series.shape[0] // wide_count
    whole_x = lax.all_to_all(series, "wide", split_axis=0, concat_axis=1, tiled=True)
    whole_cot = lax.all_to_all(cotangent, "wide", split_axis=0, concat_axis=1, tiled=True)
    own_lengths = lax.dynamic_slice_in_dim(lengths, wide_index * local_series, local_series, 0)
    if local_series % 2:
        whole_x = jnp.pad(whole_x, ((0, 1), (0, 0), (0, 0)))
        whole_cot = jnp.pad(whole_cot, ((0, 1), (0, 0), (0, 0)))
        own_lengths = jnp.pad(own_lengths, (0, 1))
    rank = jnp.sum(freqs[:, None] > freqs[None, :], axis=1)
    at = jnp.arange(K)
    ascending = jnp.sum(jnp.where(rank[:, None] == at[None, :], freqs[:, None], 0), axis=0)

    def pack(v):
        return v.transpose(1, 0, 2).reshape(v.shape[1], 2 * C)

    def unpack(v):
        return v.reshape(v.shape[0], 2, C).transpose(1, 0, 2)

    outs, gsers = [], []
    gm1, gm2, small_grad = 0.0, 0.0, 0.0
    for pair in range(whole_x.shape[0] // 2):
        cut = slice(2 * pair, 2 * pair + 2)
        out, gser, g1, g2, gs = run_block(
            pack(whole_x[cut]), pack(whole_cot[cut]), own_lengths[cut], ascending, w1, w2, small
        )
        outs.append(unpack(out))
        gsers.append(unpack(gser))
        gm1, gm2, small_grad = gm1 + g1, gm2 + g2, small_grad + gs
    output_whole = jnp.concatenate(outs)[:local_series]
    grad_whole = jnp.concatenate(gsers)[:local_series]
    output_shards = lax.all_to_all(output_whole, "wide", split_axis=1, concat_axis=0, tiled=True)
    grad_shards = lax.all_to_all(grad_whole, "wide", split_axis=1, concat_axis=0, tiled=True)

    cells = jnp.concatenate([from_matrix(gm1), from_matrix(gm2)], axis=0)
    cell_of = np.full(count * room, 2 * CELLS)
    cell_of[row_of] = np.arange(2 * CELLS)
    cells = jnp.pad(cells, ((0, 1), (0, 0)))
    cells = jnp.take(cells, jnp.asarray(cell_of), axis=0)
    summed = lax.psum_scatter(cells, both, scatter_dimension=0, tiled=True) * (1.0 / NKER)
    square = jnp.sum(jnp.sum(summed * summed, axis=1) * weight_me)
    small_sum = lax.psum(small_grad, both)
    square_sum = lax.psum(square, both) + jnp.sum(small_sum * small_sum)
    back = jnp.einsum("kd,kw->dw", pick_me, summed, precision=precise)
    got = lax.all_to_all(back, both, split_axis=0, concat_axis=0, tiled=True)
    tap_grad = jnp.einsum("ot,ow->tw", spread_me, got, precision=precise)
    share_grad = lax.dynamic_slice_in_dim(tap_grad.reshape(-1), lead, share, 0)

    grad_norm = jnp.sqrt(square_sum)
    factor = jnp.minimum(1.0, clip_norm / (grad_norm + 1e-06))
    new_kernels, new_kernel_m, new_kernel_v = adam_update(
        kernels, share_grad * factor, kernel_m, kernel_v
    )
    new_small, new_small_m, new_small_v = adam_update(small, small_sum * factor, small_m, small_v)
    return (
        output_shards,
        grad_shards,
        grad_norm,
        new_kernels,
        new_kernel_m,
        new_kernel_v,
        new_small,
        new_small_m,
        new_small_v,
    )


def solution(mesh):
    placed = (
        P("batch", "wide", None),
        P("batch"),
        P(),
        P("batch", "wide", None),
        P(("wide", "batch")),
        P(("wide", "batch")),
        P(("wide", "batch")),
        P(),
        P(),
        P(),
    )
    return jax.shard_map(
        local,
        mesh=mesh,
        in_specs=placed,
        out_specs=(
            P("batch", "wide", None),
            P("batch", "wide", None),
            P(),
            P(("wide", "batch")),
            P(("wide", "batch")),
            P(("wide", "batch")),
            P(),
            P(),
            P(),
        ),
        check_vma=False,
    )
```

time: 991 us -> 660 us (0.67)
  other arithmetic: 286 us -> 9.04 us
  matrix products: 191 us -> 6.28 us
  Pallas kernels: 0 us -> 163 us
  waiting for transfers between devices: 84.1 us -> 172 us
  local copies, waits for them, and re-layouts: 277 us -> 206 us
  between operations: 63 us -> 17.4 us
    dot_general x36 -> x4, matrix products: 177 us -> 6.28 us  [the longest x1 1.96 us: local(): jnp.einsum('kd,dw->kw', pick_me, got, precision=precise) * (1.0 / NKER)]
    pallas_call x0 -> x1, Pallas kernels: none -> 163 us  [run_block(): pl.pallas_call(functools.partial(block_kernel, L), out_shape=(sds((L, 128...]
    reduce_scatter x0 -> x1, waiting for transfers between devices: none -> 120 us  [local(): lax.psum_scatter(cells, both, scatter_dimension=0, tiled=True)]
    reduce_sum x16 -> x5, other arithmetic: 87.8 us -> 2.32 us  [the longest x2 1.45 us: local(): square = jnp.sum(jnp.sum(summed * summed, axis=1) * weight_me)]
    psum x1 -> x0, waiting for transfers between devices: 75.9 us -> none  [local(): full_grad, small_sum = lax.psum((flat_grad, small_grad), ('wide', 'batch'))]
    unnamed x244 -> x0, other arithmetic: 70.9 us -> none
    concatenate x0 -> x11, local copies, waits for them, and re-layouts: none -> 65.1 us  [the longest x2 29.3 us: from_matrix(): grid = jnp.concatenate([grid[o:o + 1] for o in SLOT_OF], axis=0)]
    and x77 -> x0, other arithmetic: 60.3 us -> none  [the longest x27 21.9 us: column_shifts(): inside = (within + col_off >= 0) & (within + col_off < period)]
  transfers between devices with their start and end apart: 6 -> 7, of which waited for: 2 -> 5; matrix products, arithmetic and copies ran while one was open for 42% -> 3% of each run, Pallas kernels for 0% -> 0%
where the time goes in v1:
time: 660 us; the launch traced here: 653 us
  local copies, waits for them, and re-layouts  206 us (31%)
  waiting for transfers between devices  172 us (26%)
  Pallas kernels  163 us (25%)
  blocking collectives  63.4 us (10%)
  between operations  17.4 us (3%)
  starting transfers between devices  16.5 us (2%)
  other arithmetic  9.04 us (1%)
    pallas_call x1, Pallas kernels, run_block(): pl.pallas_call(functools.partial(block_kernel, L), out_shape=(sds((L, 128...  163 us
    reduce_scatter x1, waiting for transfers between devices, local(): lax.psum_scatter(cells, both, scatter_dimension=0, tiled=True)  120 us
    slice x24, local copies, waits for them, and re-layouts, to_matrix(): grid = jnp.concatenate([grid[o:o + 1] for o in CELL_OF], axis=0)  44.9 us
    psum x1, blocking collectives, local(): square_sum = lax.psum(square, both) + jnp.sum(small_sum * small_sum)  40.8 us
    concatenate x2, local copies, waits for them, and re-layouts, from_matrix(): grid = jnp.concatenate([grid[o:o + 1] for o in SLOT_OF], axis=0)  29.3 us
    concatenate x2, local copies, waits for them, and re-layouts, to_matrix(): grid = jnp.concatenate([grid[o:o + 1] for o in CELL_OF], axis=0)  26.6 us
    all_gather x1, waiting for transfers between devices, local(): merged = lax.all_gather(merged.astype(bf16), both, axis=0, tiled=True)  23.1 us
    all_to_all x1, blocking collectives, local(): got = lax.all_to_all(slots, both, split_axis=0, concat_axis=0, tiled=True)  22.6 us
  transfers between devices with their start and end apart: 7, of which 5 were waited for; matrix products, arithmetic and copies ran while one was open for 3% of the time, Pallas kernels for 0%

profile of v1, /device:TPU:0, one launch (start us, length us, event | category | flops | bytes accessed | tf_op | source)
XLA Modules:
  0.0 653.2 jit_solution(16382417651736883404)
XLA Ops:
  7.3 3.4 dynamic_update_slice.3
  10.8 1.3 convolution_bitcast_fusion.1
  12.6 22.6 %all_to_all.96 = f32[32,1,4096]{2,1,0:T(1,128)S(1)} all-to-all(f32[32,1,4096]{2,1,0:T(1,128)S(1)} %copy.123), channel_id=1, replica_groups=mesh['wide'=4,'batch'=8] {'wide','batch'}, dimensions={0} | all-to-all | bytes 1048576 | tf_op jit(solution)/shard_map/all_to_all | solution.py:611
  35.3 2.0 fusion
  37.3 3.5 all-to-all-start
  41.3 12.2 %all-to-all-done = bf16[8,264,64]{1,2,0:T(8,128)(2,1)S(1)} async-done(((bf16[8,264,64]{1,2,0:T(8,128)(2,1)}), bf16[8,264,64]{1,2,0:T(8,128)(2,1)S(1)}, u32[]{:S(2)}, u32[]{:S(2)}) %all-to-all-start) | async-done | bytes 270368 | tf_op jit(solution)/shard_map/all_to_all | solution.py:619
  53.5 3.5 all-to-all-start.1
  60.7 8.3 %all-to-all-done.1 = bf16[8,264,64]{1,2,0:T(8,128)(2,1)S(1)} async-done(((bf16[8,264,64]{1,2,0:T(8,128)(2,1)}), bf16[8,264,64]{1,2,0:T(8,128)(2,1)S(1)}, u32[]{:S(2)}, u32[]{:S(2)}) %all-to-all-start.1) | async-done | bytes 270368 | tf_op jit(solution)/shard_map/all_to_all | solution.py:620
  70.5 23.1 %all-gather.2.cloned.1.call-done = bf16[256,4096]{1,0:T(8,128)(2,1)} async-done(((bf16[8,4096]{1,0:T(8,128)(2,1)}), bf16[256,4096]{1,0:T(8,128)(2,1)}) %all-gather.2.cloned.1.call-update) | async-done | bytes 2097168 | tf_op jit(solution)/shard_map/all_gather | solution.py:613
  93.7 5.6 gather_fusion
  99.2 1.3 fusion.38
  101.4 1.6 slice.403
  103.0 2.0 slice.404
  105.0 2.0 slice.405
  107.1 2.0 slice.406
  117.4 13.3 %concatenate.47 = bf16[11,11,64,64]{3,0,2,1:T(8,128)(2,1)S(1)} concatenate(bf16[1,11,64,64]{3,0,2,1:T(2,128)(2,1)S(1)} %slice.403, bf16[1,11,64,64]{3,0,2,1:T(2,128)(2,1)} %slice.404, bf16[1,11,64,64]{3,0,2,1:T(2,128)(2,1)} %slice.405, bf16[1,11,64,64]{3,0,2,1:T(2,128)(2,1)} %slice.406, bf16[1,11,64,64]{3,0,2,1:T(2,128)(2,1)} %slice.407, bf16[1,11,64,64]{3,0,2,1:T(2,128)(2,1)} %slice.408, ...), dimensions={0} | concatenate | bytes 1982464 | tf_op jit(solution)/shard_map/concatenate | solution.py:583
  131.2 1.6 copy-done.1
  132.8 4.5 reshape.106
  137.3 1.4 slice.394
  138.7 2.0 slice.395
  142.0 1.2 slice.397
  149.1 1.2 slice.392
  150.3 13.8 %slice.393 = bf16[1,11,64,64]{3,0,2,1:T(2,128)(2,1)} reshape(bf16[11,4096]{1,0:T(8,128)(2,1)S(1)} %copy-done.12) | data formatting | bytes 180224 | tf_op jit(solution)/shard_map/slice | solution.py:583
  164.1 13.3 %concatenate.45 = bf16[11,11,64,64]{3,0,2,1:T(8,128)(2,1)S(1)} concatenate(bf16[1,11,64,64]{3,0,2,1:T(2,128)(2,1)} %slice.392, bf16[1,11,64,64]{3,0,2,1:T(2,128)(2,1)} %slice.393, bf16[1,11,64,64]{3,0,2,1:T(2,128)(2,1)S(1)} %slice.394, bf16[1,11,64,64]{3,0,2,1:T(2,128)(2,1)} %slice.395, bf16[1,11,64,64]{3,0,2,1:T(2,128)(2,1)} %slice.396, bf16[1,11,64,64]{3,0,2,1:T(2,128)(2,1)} %slice.397, ...), dimensions={0} | concatenate | bytes 1982464 | tf_op jit(solution)/shard_map/concatenate | solution.py:583
  177.8 1.6 copy-done.2
  179.4 3.6 reshape.105
  183.0 2.4 pad.21.w2_ref
  186.5 162.6 %block.1 = (bf16[1056,128]{1,0:T(8,128)(2,1)}, bf16[1056,128]{1,0:T(8,128)(2,1)}, f32[768,768]{1,0:T(8,128)}, f32[768,768]{1,0:T(8,128)}, f32[4,128]{1,0:T(4,128)}) custom-call(s32[5]{0:T(128)} %copy-done.20, s32[2]{0:T(128)} %dynamic_slice.18.len_ref, bf16[1056,128]{1,0:T(8,128)(2,1)} %copy.146.x_ref, bf16[1056,128]{1,0:T(8,128)(2,1)} %copy.147.cot_ref, ...), custom_call_target="tpu_custom_call" | custom-call | tf_op jit(solution)/shard_map/block/pallas_call | solution.py:526
  349.1 1.7 slice.369
  350.9 3.1 reshape.110
  354.0 5.6 fusion.36
  359.6 3.3 slice.452
  362.9 2.9 slice.454
  366.0 3.1 reshape.112
  369.2 5.6 fusion.37
  374.8 2.2 slice.462
  377.0 2.9 slice.464
  379.9 14.5 %concatenate.50 = f32[11,11,64,64]{3,0,2,1:T(8,128)} concatenate(f32[2,11,64,64]{3,0,2,1:T(2,128)} %get-tuple-element.29, f32[2,11,64,64]{3,0,2,1:T(2,128)} %get-tuple-element.28, f32[4,11,64,64]{3,0,2,1:T(4,128)S(1)} %copy-done, f32[2,11,64,64]{3,0,2,1:T(2,128)} %get-tuple-element.27, f32[1,11,64,64]{3,0,2,1:T(1,128)S(1)} %copy-done.4), dimensions={0} | concatenate | bytes 3964928 | tf_op jit(solution)/shard_map/concatenate | solution.py:591
  394.4 1.3 slice_dynamic-update-slice_fusion.7
  395.7 1.3 slice_dynamic-update-slice_fusion.6
  397.0 1.7 slice_dynamic-update-slice_fusion.1
  398.7 1.3 slice_dynamic-update-slice_fusion.5
  401.1 3.1 copy.155
  404.2 3.4 reshape.111
  407.7 14.7 %concatenate.52 = f32[11,11,64,64]{3,0,2,1:T(8,128)} concatenate(f32[2,11,64,64]{3,0,2,1:T(2,128)} %get-tuple-element.32, f32[2,11,64,64]{3,0,2,1:T(2,128)} %get-tuple-element.31, f32[4,11,64,64]{3,0,2,1:T(4,128)S(1)} %slice.462, f32[2,11,64,64]{3,0,2,1:T(2,128)} %get-tuple-element.30, f32[1,11,64,64]{3,0,2,1:T(1,128)} %slice.464), dimensions={0} | concatenate | bytes 3964928 | tf_op jit(solution)/shard_map/concatenate | solution.py:591
  422.4 1.3 slice_dynamic-update-slice_fusion.4
  423.7 1.3 slice_dynamic-update-slice_fusion.3
  425.0 1.7 slice_dynamic-update-slice_fusion
  426.8 1.3 slice_dynamic-update-slice_fusion.2
  429.1 3.1 copy.156
  432.2 4.5 reshape.113
  436.8 4.0 select_maximum_fusion
  440.7 7.8 %gather_fusion.1 = f32[256,4096]{1,0:T(8,128)} fusion(f32[243,4096]{1,0:T(8,128)} %select_maximum_fusion, s32[1024]{0:T(1024)S(1)} %pad_clamp_fusion), kind=kCustom, calls=%fused_computation.1 | custom fusion | bytes 8389632 | tf_op jit(solution)/shard_map/jit(_take)/gather | solution.py:655
  451.7 3.5 all-to-all-start.3
  457.5 8.3 %all-to-all-done.3 = bf16[4,2,16896]{2,1,0:T(2,128)(2,1)S(1)} async-done(((bf16[4,2,16896]{2,1,0:T(2,128)(2,1)}), bf16[4,2,16896]{2,1,0:T(2,128)(2,1)S(1)}, u32[]{:S(2)}, u32[]{:S(2)}) %all-to-all-start.3) | async-done | bytes 270368 | tf_op jit(solution)/shard_map/all_to_all | solution.py:648
  465.8 3.5 all-to-all-start.4
  469.2 119.6 %reduce-scatter.2.cloned.1.call-done = f32[8,4096]{1,0:T(8,128)} async-done(((f32[256,4096]{1,0:T(8,128)}), f32[8,4096]{1,0:T(8,128)}) %reduce-scatter.2.cloned.1.call-update) | async-done | bytes 131088 | tf_op jit(solution)/shard_map/reduce_scatter | solution.py:656
  588.9 1.6 convolution_bitcast_fusion
  590.5 1.3 copy.157
  591.8 2.6 all-to-all-start.5
  596.5 1.3 fusion.32
  598.9 40.8 %all-reduce.5 = (f32[]{:T(128)}, f32[256]{0:T(256)S(1)}) all-reduce(f32[]{:T(128)} %fusion.32, f32[256]{0:T(256)S(1)} %reshape.114), channel_id=1, replica_groups=mesh['wide'=4,'batch'=8] {'wide','batch'}, use_global_device_ids=true, to_apply=%region_5.6 | all-reduce | flops 257 | bytes 2056 | tf_op jit(solution)/shard_map/psum | solution.py:659
  642.2 1.5 fusion.1
  643.8 1.2 multiply_subtract_fusion
  (123 shorter events, 36.7 us)
Async XLA Ops:
  7.2 86.5 %all-gather.2.cloned.1.call-start = ((), (), s32[]{:S(2)}) async-start(), calls=%async_computation.7 | async-start | bytes 2162688 | tf_op jit(solution)/shard_map/all_gather | solution.py:613
  7.3 33.5 %copy-start.26 = (s32[5]{0:T(128)S(1)}, s32[5]{0:T(128)}, u32[]{:S(2)}) copy-start(s32[5]{0:T(128)} %param.17) | copy-start | bytes 64
  10.8 47.2 %copy-start.19 = (f32[256]{0:T(256)S(1)}, f32[256]{0:T(256)}, u32[]{:S(2)}) copy-start(f32[256]{0:T(256)} %param.22) | copy-start | bytes 3076
  10.8 47.2 %copy-start.27 = (s32[8]{0:T(128)S(1)}, s32[8]{0:T(128)}, u32[]{:S(2)}) copy-start(s32[8]{0:T(128)} %param.16) | copy-start | bytes 100
  10.8 48.5 %copy-start.25 = (s32[242]{0:T(256)S(1)}, s32[242]{0:T(256)}, u32[]{:S(2)}) copy-start(s32[242]{0:T(256)} %constant.167) | copy-start | bytes 2908
  10.8 48.5 %copy-start.24 = (s32[256]{0:T(256)S(1)}, s32[256]{0:T(256)}, u32[]{:S(2)}) copy-start(s32[256]{0:T(256)} %constant.168) | copy-start | bytes 3076
  37.3 16.3 %all-to-all-start = ((bf16[8,264,64]{1,2,0:T(8,128)(2,1)}), bf16[8,264,64]{1,2,0:T(8,128)(2,1)S(1)}, u32[]{:S(2)}, u32[]{:S(2)}) async-start(bf16[8,264,64]{1,2,0:T(8,128)(2,1)} %param.15), calls=%async_computation | async-start | bytes 786432 | tf_op jit(solution)/shard_map/all_to_all | solution.py:619
  41.0 29.5 %copy-start.20 = (s32[5]{0:T(128)}, s32[5]{0:T(128)S(1)}, u32[]{:S(2)}) copy-start(s32[5]{0:T(128)S(1)} %select_reduce_fusion.freq_ref) | copy-start | bytes 64
  53.5 15.5 %all-to-all-start.1 = ((bf16[8,264,64]{1,2,0:T(8,128)(2,1)}), bf16[8,264,64]{1,2,0:T(8,128)(2,1)S(1)}, u32[]{:S(2)}, u32[]{:S(2)}) async-start(bf16[8,264,64]{1,2,0:T(8,128)(2,1)} %param.18), calls=%async_computation.1 | async-start | bytes 786432 | tf_op jit(solution)/shard_map/all_to_all | solution.py:620
  57.0 531.9 %reduce-scatter.2.cloned.1.call-start = ((), (), s32[]{:S(2)}) async-start(), calls=%async_computation.8 | async-start | bytes 4325376 | tf_op jit(solution)/shard_map/reduce_scatter | solution.py:656
  101.4 14.8 %copy-start.14 = (bf16[11,4096]{1,0:T(8,128)(2,1)S(1)}, bf16[11,4096]{1,0:T(8,128)(2,1)}, u32[]{:S(2)}) copy-start(bf16[11,4096]{1,0:T(8,128)(2,1)} %get-tuple-element.52) | copy-start | bytes 270340
  131.2 1.6 copy-start.1
  132.7 8.0 %copy-start.10 = (bf16[11,4096]{1,0:T(8,128)(2,1)S(1)}, bf16[11,4096]{1,0:T(8,128)(2,1)}, u32[]{:S(2)}) copy-start(bf16[11,4096]{1,0:T(8,128)(2,1)} %get-tuple-element.49) | copy-start | bytes 270340
  132.7 9.2 %copy-start.9 = (bf16[11,4096]{1,0:T(8,128)(2,1)S(1)}, bf16[11,4096]{1,0:T(8,128)(2,1)}, u32[]{:S(2)}) copy-start(bf16[11,4096]{1,0:T(8,128)(2,1)} %get-tuple-element.48) | copy-start | bytes 270340
  132.8 10.4 %copy-start.8 = (bf16[11,4096]{1,0:T(8,128)(2,1)S(1)}, bf16[11,4096]{1,0:T(8,128)(2,1)}, u32[]{:S(2)}) copy-start(bf16[11,4096]{1,0:T(8,128)(2,1)} %get-tuple-element.47) | copy-start | bytes 270340
  132.8 11.6 %copy-start.7 = (bf16[11,4096]{1,0:T(8,128)(2,1)S(1)}, bf16[11,4096]{1,0:T(8,128)(2,1)}, u32[]{:S(2)}) copy-start(bf16[11,4096]{1,0:T(8,128)(2,1)} %get-tuple-element.46) | copy-start | bytes 270340
  132.8 12.8 %copy-start.6 = (bf16[11,4096]{1,0:T(8,128)(2,1)S(1)}, bf16[11,4096]{1,0:T(8,128)(2,1)}, u32[]{:S(2)}) copy-start(bf16[11,4096]{1,0:T(8,128)(2,1)} %get-tuple-element.45) | copy-start | bytes 270340
  137.3 11.8 %copy-start.13 = (bf16[11,4096]{1,0:T(8,128)(2,1)S(1)}, bf16[11,4096]{1,0:T(8,128)(2,1)}, u32[]{:S(2)}) copy-start(bf16[11,4096]{1,0:T(8,128)(2,1)} %get-tuple-element.54) | copy-start | bytes 270340
  137.3 13.0 %copy-start.12 = (bf16[11,4096]{1,0:T(8,128)(2,1)S(1)}, bf16[11,4096]{1,0:T(8,128)(2,1)}, u32[]{:S(2)}) copy-start(bf16[11,4096]{1,0:T(8,128)(2,1)} %get-tuple-element.53) | copy-start | bytes 270340
  177.8 1.6 copy-start.2
  359.6 6.3 copy-start.3
  374.8 5.1 copy-start
  374.8 5.1 copy-start.4
  448.5 1.0 copy-start.18
  448.5 6.7 %copy-start.17 = (bf16[1056,128]{1,0:T(8,128)(2,1)S(1)}, bf16[1056,128]{1,0:T(8,128)(2,1)}, u32[]{:S(2)}) copy-start(bf16[1056,128]{1,0:T(8,128)(2,1)} %get-tuple-element.15) | copy-start | bytes 811012
  451.7 14.1 %all-to-all-start.3 = ((bf16[4,2,16896]{2,1,0:T(2,128)(2,1)}), bf16[4,2,16896]{2,1,0:T(2,128)(2,1)S(1)}, u32[]{:S(2)}, u32[]{:S(2)}) async-start(bf16[4,2,16896]{2,1,0:T(2,128)(2,1)} %reshape.132), calls=%async_computation.3 | async-start | bytes 540672 | tf_op jit(solution)/shard_map/all_to_all | solution.py:648
  455.2 139.3 %copy-start.21 = (f32[4,128]{1,0:T(4,128)S(1)}, f32[4,128]{1,0:T(4,128)}, u32[]{:S(2)}) copy-start(f32[4,128]{1,0:T(4,128)} %get-tuple-element.18) | copy-start | bytes 6148
  465.8 126.0 %all-to-all-start.4 = ((bf16[4,2,16896]{2,1,0:T(2,128)(2,1)}), bf16[4,2,16896]{2,1,0:T(2,128)(2,1)S(1)}, u32[]{:S(2)}, u32[]{:S(2)}) async-start(bf16[4,2,16896]{2,1,0:T(2,128)(2,1)} %reshape.134), calls=%async_computation.4 | async-start | bytes 540672 | tf_op jit(solution)/shard_map/all_to_all | solution.py:649
  588.9 7.5 %copy-start.11 = (f32[8,4096]{1,0:T(8,128)S(1)}, f32[8,4096]{1,0:T(8,128)}, u32[]{:S(2)}) copy-start(f32[8,4096]{1,0:T(8,128)} %reduce-scatter.2.cloned.1.call-done) | copy-start | bytes 393220
  590.5 51.2 %copy-start.22 = (f32[256]{0:T(256)S(1)}, f32[256]{0:T(256)}, u32[]{:S(2)}) copy-start(f32[256]{0:T(256)} %param.23) | copy-start | bytes 3076
  590.5 51.2 %copy-start.23 = (f32[256]{0:T(256)S(1)}, f32[256]{0:T(256)}, u32[]{:S(2)}) copy-start(f32[256]{0:T(256)} %param.24) | copy-start | bytes 3076
  591.8 50.4 %all-to-all-start.5 = ((f32[32,1,4096]{2,1,0:T(1,128)}), f32[32,1,4096]{2,1,0:T(1,128)S(1)}, u32[]{:S(2)}, u32[]{:S(2)}) async-start(f32[32,1,4096]{2,1,0:T(1,128)} %copy.157), calls=%async_computation.6 | async-start | bytes 1048576 | tf_op jit(solution)/shard_map/all_to_all | solution.py:661
  594.4 49.3 %copy-start.5 = (f32[73216]{0:T(1024)S(1)}, f32[73216]{0:T(1024)}, u32[]{:S(2)}) copy-start(f32[73216]{0:T(1024)} %param.19) | copy-start | bytes 878596
  594.4 49.3 %copy-start.15 = (f32[73216]{0:T(1024)S(1)}, f32[73216]{0:T(1024)}, u32[]{:S(2)}) copy-start(f32[73216]{0:T(1024)} %param.20) | copy-start | bytes 878596
  594.5 49.3 %copy-start.16 = (f32[73216]{0:T(1024)S(1)}, f32[73216]{0:T(1024)}, u32[]{:S(2)}) copy-start(f32[73216]{0:T(1024)} %param.21) | copy-start | bytes 878596
Sparse Core Ops, SparseCore 0:
  37.4 56.2 all-gather.1
  448.7 140.1 reduce-scatter.1
